TPU v7x, 768 devices: a whole 4x8x12 slice. The times are simulated.
768 devices in a mesh: row: 24 (over z_lo, x), col: 32 (over y, z_hi, core).
Axes of the slice: x: 4, y: 8, z: 12 (z_hi: 2, z_lo: 6; z = z_hi * 6 + z_lo), core: 2. Of those that a mesh axis runs over, the one named last changes fastest.
Arguments:
- values: bfloat16 [24576, 24576], P('row', 'col'), may hold values from -1.5 to 1.5
- pattern: int32 [96, 96], P('row', 'col'), may hold values from 0 to 1, as said below
- sections: int32 [4], replicated, may hold values from 0 to 95
Outputs:
- exposure: bfloat16 [24576, 24576], P('row', 'col')
Inputs may be any that keep to these rules, and one draw needn't show every extreme that they name: `pattern`: 1 where a tile is stored, else 0; the share of stored tiles differs from tile row to tile row.
All inputs are finite; a program needn't handle non-finite values.
Results may differ from a plain program's by a relative error of at most 0.001.
Values may be sent and summed in bfloat16 or wider, within the bound.
A program may use at most 64 MiB of HBM per device.

v0:
```python
import jax
import jax.numpy as jnp
from jax import lax
from jax.sharding import PartitionSpec as P

TILE = 256
SECTIONS = 4


def broadcast(array, axis, root):
    mine = lax.axis_index(axis) == root
    return lax.psum(jnp.where(mine, array, jnp.zeros_like(array)), axis)


def shards(values, pattern, sections):
    row_tiles, col_tiles = pattern.shape
    tile_flags = pattern.astype(jnp.bfloat16)
    accumulated = jnp.zeros(values.shape, jnp.float32)
    for section_number in range(SECTIONS):
        section_index = sections[section_number]
        local_col = section_index % col_tiles
        piece = lax.dynamic_slice_in_dim(values, local_col * TILE, TILE, 1)
        piece_flags = lax.dynamic_slice_in_dim(tile_flags, local_col, 1, 1)[:, 0]
        piece = (piece.reshape(row_tiles, TILE, TILE) * piece_flags[:, None, None]).reshape(
            row_tiles * TILE, TILE
        )
        left_panel = broadcast(piece, "col", section_index // col_tiles)
        local_row = section_index % row_tiles
        right_piece = lax.dynamic_slice_in_dim(values, local_row * TILE, TILE, 0)
        right_piece_flags = lax.dynamic_slice_in_dim(tile_flags, local_row, 1, 0)[0]
        right_panel = broadcast(
            (right_piece.reshape(TILE, col_tiles, TILE) * right_piece_flags[None, :, None]).reshape(
                TILE, col_tiles * TILE
            ),
            "row",
            section_index // row_tiles,
        )
        accumulated = accumulated + jnp.dot(
            left_panel, right_panel, preferred_element_type=jnp.float32
        )
    return accumulated.astype(jnp.bfloat16)


def solution(mesh):
    in_specs = (P("row", "col"), P("row", "col"), P())
    out_specs = P("row", "col")
    return jax.shard_map(shards, mesh=mesh, in_specs=in_specs, out_specs=out_specs, check_vma=False)
```

profile of v0, /device:TPU:66, one launch (start us, length us, event | category | flops | bytes accessed | tf_op | source)
XLA Modules:
  0.0 812.8 jit_solution(17318585819007959155)
XLA Ops:
  6.5 0.0 copy-start
  6.5 0.0 all-reduce.7.cloned.1.call-start
  6.5 1.5 fusion.8
  18.4 0.7 convert_element_type.6
  19.1 0.1 mul.188
  19.2 0.1 mul.164
  19.3 0.1 mul.152
  19.4 0.1 mul.176
  19.5 2.8 multiply_select_fusion.4
  22.3 0.0 all-reduce.7.cloned.1.call-update
  22.3 0.0 all-reduce.5.cloned.1.call-start
  27.7 0.2 fusion.3
  27.9 0.1 broadcast_bitcast_fusion
  28.0 0.1 broadcast_bitcast_fusion.2
  28.1 0.0 copy-done
  28.1 1.9 multiply_select_fusion
  30.0 0.0 all-reduce.5.cloned.1.call-update
  30.0 297.0 %all-reduce.7.cloned.1.call-done = (bf16[256,768]{1,0:T(8,128)(2,1)}, bf16[256,768]{1,0:T(8,128)(2,1)}, bf16[256,768]{1,0:T(8,128)(2,1)}, bf16[256,768]{1,0:T(8,128)(2,1)}) async-done(((bf16[256,768]{1,0:T(8,128)(2,1)}, bf16[256,768]{1,0:T(8,128)(2,1)}, bf16[256,768]{1,0:T(8,128)(2,1)}, bf16[256,768]{1,0:T(8,128)(2,1)}), (bf16[256,768]{1,0:T(8,128)(2,1)}, bf16[256,768]{1,0:T(8,128)(2,1)}, ...) | async-done | bytes 1572880 | tf_op jit(solution)/shard_map/psum | solution.py:12
  327.0 0.0 copy-start.6
  327.0 474.1 %all-reduce.5.cloned.1.call-done = (bf16[1024,256]{1,0:T(8,128)(2,1)}, bf16[1024,256]{1,0:T(8,128)(2,1)}, bf16[1024,256]{1,0:T(8,128)(2,1)}, bf16[1024,256]{1,0:T(8,128)(2,1)}) async-done(((bf16[1024,256]{1,0:T(8,128)(2,1)}, bf16[1024,256]{1,0:T(8,128)(2,1)}, bf16[1024,256]{1,0:T(8,128)(2,1)}, bf16[1024,256]{1,0:T(8,128)(2,1)}), (bf16[1024,256]{1,0:T(8,128)(2,1)}, bf16[1024,256]{1,0:T(8,128)(2,1)}, ...) | async-done | bytes 2097168 | tf_op jit(solution)/shard_map/psum | solution.py:12
  801.1 0.0 copy-start.3
  801.1 0.0 copy-start.2
  801.1 0.0 copy-start.5
  801.2 1.8 fusion.11
  803.0 0.0 copy-done.6
  803.0 0.0 copy-done.3
  803.0 0.0 copy-start.1
  803.0 0.0 copy-start.4
  803.0 0.6 fusion.9
  803.6 0.0 copy-done.2
  803.6 0.0 copy-done.5
  803.6 0.6 fusion.10
  804.2 0.0 copy-done.1
  804.2 0.0 copy-done.4
  804.2 1.7 add_convert_fusion
  (9 shorter events, 0.1 us)
Async XLA Ops:
  6.5 21.5 %copy-start = (bf16[1024,768]{1,0:T(8,128)(2,1)S(1)}, bf16[1024,768]{1,0:T(8,128)(2,1)}, u32[]{:S(2)}) copy-start(bf16[1024,768]{1,0:T(8,128)(2,1)} %param.3) | copy-start | bytes 4718596
  6.5 320.5 %all-reduce.7.cloned.1.call-start = ((), (), s32[]{:S(2)}) async-start(), calls=%async_computation.1 | async-start | bytes 3145728 | tf_op jit(solution)/shard_map/psum | solution.py:12
  22.3 778.8 %all-reduce.5.cloned.1.call-start = ((), (), s32[]{:S(2)}) async-start(), calls=%async_computation | async-start | bytes 4194304 | tf_op jit(solution)/shard_map/psum | solution.py:12
  327.0 476.0 %copy-start.6 = (bf16[256,768]{1,0:T(8,128)(2,1)S(1)}, bf16[256,768]{1,0:T(8,128)(2,1)}, u32[]{:S(2)}) copy-start(bf16[256,768]{1,0:T(8,128)(2,1)} %get-tuple-element.14) | copy-start | bytes 1179652
  801.1 1.9 copy-start.3
  801.1 2.5 copy-start.2
  801.1 2.5 copy-start.5
  803.0 1.2 copy-start.1
  803.0 1.2 copy-start.4
Sparse Core Ops, SparseCore 0:
  22.4 304.5 all-reduce.6
  330.8 470.2 all-reduce.4
where the time goes:
time: 813 us
  waiting for transfers between devices  771 us (95%)
  between operations  29.2 us (4%)
    psum x2, waiting for transfers between devices, broadcast(): return lax.psum(jnp.where(mine, array, jnp.zeros_like(array)), axis)  771 us
  transfers between devices with their start and end apart: 2, of which 2 were waited for; matrix products, arithmetic and copies ran while one was open for 0% of the time, Pallas kernels for 0%

commit v1 on v0

v1 whole, which is shorter than its diff:
```python
import jax
import jax.numpy as jnp
from jax import lax
from jax.experimental import pallas as pl
from jax.experimental.pallas import tpu as pltpu
from jax.sharding import PartitionSpec as P

TILE = 256
SECTIONS = 4
X, Y, ZL, ZH, CORES = 4, 8, 6, 2, 2
LB = 64
RB = 64
WIDTH = 768
MESH = pl.DeviceIdType.MESH


def kernel(
    sections, pattern, values, out,
    vals, sib_out, sib_in, own, lrs, zout, zin, left, rown, rrs, rgot, flood, right,
    load_sem, xc_s, xc_r, lrs_s, lrs_r, lz_s, lz_r, lag_s, lag_r, lic_s, lic_r,
    rrs_s, rrs_r, rfl_s, rfl_r, rag_s, rag_r,
):
    row, col = lax.axis_index("row"), lax.axis_index("col")
    x, zl = row % X, row // X
    core, zh, y = col % CORES, col // CORES % ZH, col // (CORES * ZH)
    way = 1 - 2 * core

    def device(dx=0, dy=0, dzl=0, dzh=0, dcore=0):
        r = (zl + dzl) * X + (x + dx + X) % X
        c = ((y + dy + Y) % Y) * (ZH * CORES) + (zh + dzh) % ZH * CORES + (core + dcore) % CORES
        return (r, c)

    def copy(src, dst, send, recv, to):
        return pltpu.make_async_remote_copy(
            src_ref=src, dst_ref=dst, send_sem=send, recv_sem=recv, device_id=to, device_id_type=MESH
        )

    x_fwd, x_back = device(dx=way), device(dx=-way)
    y_fwd, y_back = device(dy=way), device(dy=-way)
    z_far, sibling = device(dzh=1), device(dcore=1)
    z_up, z_down = device(dzl=1), device(dzl=-1)

    load = pltpu.make_async_copy(values, vals, load_sem)
    load.start()
    barrier = pltpu.get_barrier_semaphore()
    for to in (x_fwd, x_back, y_fwd, y_back, z_far, sibling):
        pl.semaphore_signal(barrier, inc=1, device_id=to, device_id_type=MESH)

    @pl.when(zl > 0)
    def _():
        pl.semaphore_signal(barrier, inc=1, device_id=z_down, device_id_type=MESH)

    @pl.when(zl < ZL - 1)
    def _():
        pl.semaphore_signal(barrier, inc=1, device_id=z_up, device_id_type=MESH)

    load.wait()

    def each(body):
        def step(s, carry):
            body(s)
            return carry
        lax.fori_loop(0, SECTIONS, step, 0)

    def lcol(s):
        return sections[s] // 3

    def lroot(s):
        c = lcol(s)
        return c // (CORES * ZH), c // CORES % ZH, c % CORES

    def rroot(s):
        r = sections[s] // 4
        return r % X, r // X

    def factor(condition, scale=1):
        return (condition.astype(jnp.int32) * scale).astype(jnp.float32).astype(jnp.bfloat16)

    def pick(*choices):
        total = None
        for condition, array in choices:
            term = array * factor(condition)
            total = term if total is None else total + term
        return total

    def left_half(half, dst, s):
        lc = sections[s] % 3

        def block(b, carry):
            rows = pl.ds(pl.multiple_of(half * 512 + b * LB, LB), LB)
            total = None
            for k in range(3):
                term = vals[rows, k * TILE : (k + 1) * TILE] * factor(
                    lc == k, pattern[half * 2 + b // 4, k]
                )
                total = term if total is None else total + term
            dst[s, b] = total
            return carry
        lax.fori_loop(0, Y, block, 0)

    def right_piece(s):
        lr = sections[s] % 4
        for k in range(3):
            lanes = slice(k * TILE, (k + 1) * TILE)
            factors = [factor(lr == r, pattern[r, k]) for r in range(4)]

            def block(b, carry):
                total = None
                for r in range(4):
                    rows = pl.ds(pl.multiple_of(r * TILE + b * RB, RB), RB)
                    term = vals[rows, lanes] * factors[r]
                    total = term if total is None else total + term
                rown[s, b, :, lanes] = total
                return carry
            lax.fori_loop(0, X, block, 0)

    def sib_copy(s):
        return copy(sib_out.at[s], sib_in.at[s], xc_s.at[s], xc_r.at[s], sibling)

    each(lambda s: left_half(1 - core, sib_out, s))
    n_z = jnp.where(zl > 0, 1, 0) + jnp.where(zl < ZL - 1, 1, 0)
    pl.semaphore_wait(barrier, 6 + n_z)
    each(lambda s: sib_copy(s).start())

    def rrs_copy(k, s):
        if k == 0:
            src, to = rown.at[s, (x + 2) % X], x_fwd
        elif k == 1:
            src, to = rrs.at[0, s], x_fwd
        else:
            src, to = rown.at[s, (x - way + X) % X], x_back
        return copy(src, rrs.at[k, s], rrs_s.at[k, s], rrs_r.at[k, s], to)

    def right_first(s):
        right_piece(s)
        rrs_copy(0, s).start()
        rrs_copy(2, s).start()
    each(right_first)

    each(lambda s: left_half(core, own, s))

    def lrs_copy(k, s):
        if k < 4:
            src = own.at[s, (y + 4) % Y] if k == 0 else lrs.at[k - 1, s]
            to = y_fwd
        else:
            src = own.at[s, (y - 3 * way + Y) % Y] if k == 4 else lrs.at[k - 1, s]
            to = y_back
        return copy(src, lrs.at[k, s], lrs_s.at[k, s], lrs_r.at[k, s], to)

    def left_first(s):
        sib_copy(s).wait_recv()
        root = lroot(s)[2]
        mine = root == core

        def block(b, carry):
            own[s, b] = pick((mine, own[s, b]), (root != core, sib_in[s, b]))
            return carry
        lax.fori_loop(0, Y, block, 0)
        lrs_copy(0, s).start()
        lrs_copy(4, s).start()
    each(left_first)

    def right_second(s):
        rrs_copy(0, s).wait_recv()
        root = rroot(s)[0]
        rrs[0, s] = pick((root == x, rown[s, (x + way + X) % X]), (root != x, rrs[0, s]))
        rrs_copy(1, s).start()
    each(right_second)

    def left_step(h):
        def body(s):
            root = lroot(s)[0]
            lrs_copy(h - 1, s).wait_recv()
            lrs[h - 1, s] = pick(
                (root == y, own[s, (y + (4 - h) * way + Y) % Y]), (root != y, lrs[h - 1, s])
            )
            lrs_copy(h, s).start()
            if h < 3:
                lrs_copy(3 + h, s).wait_recv()
                lrs[3 + h, s] = pick(
                    (root == y, own[s, (y - (3 - h) * way + Y) % Y]), (root != y, lrs[3 + h, s])
                )
                lrs_copy(4 + h, s).start()
        each(body)

    left_step(1)

    def right_third(s):
        rrs_copy(1, s).wait_recv()
        rrs_copy(2, s).wait_recv()
        delta = ((rroot(s)[0] - x) * way + X) % X
        rgot[s] = pick((delta == 0, rown[s, x]), (delta == 1, rrs[2, s]), (delta >= 2, rrs[1, s]))

    first = zl // 3
    place = jnp.where(first == 0, zl, ZL - 1 - zl)
    second = 1 - first

    def flood_copy(k, s, up):
        return copy(
            flood.at[k, s], flood.at[k, s], rfl_s.at[k, s], rfl_r.at[k, s],
            device(dzl=up),
        )

    def flow_first(at):
        @pl.when(place == at)
        def _():
            def body(s):
                if at == 0:
                    flood[first, s] = rgot[s]
                else:
                    flood_copy(first, s, 1 - 2 * first).wait_recv()
                    root = rroot(s)[1]
                    flood[first, s] = pick((root == zl, rgot[s]), (root != zl, flood[first, s]))
                flood_copy(first, s, 1 - 2 * first).start()
            each(body)

    def rag_copy(k, s):
        block = (x - way + X) % X if k == 1 else x
        to = x_back if k == 2 else x_fwd
        return copy(
            right.at[s, block], right.at[s, block], rag_s.at[k, s], rag_r.at[k, s], to
        )

    def rag_wait(k, s):
        block = [(x - way + X) % X, (x + 2) % X, (x + way + X) % X][k]
        copy(right.at[s, block], right.at[s, block], rag_s.at[k, s], rag_r.at[k, s], x_fwd).wait_recv()

    def flow_second(at):
        @pl.when(place == 5 - at)
        def _():
            def body(s):
                flood_copy(second, s, 2 * first - 1).wait_recv()
                root = rroot(s)[1]
                flood[second, s] = pick((root == zl, rgot[s]), (root != zl, flood[second, s]))
                if at < 5:
                    flood_copy(second, s, 2 * first - 1).start()
                right[s, x] = pick((root <= zl, flood[0, s]), (root > zl, flood[1, s]))
                rag_copy(0, s).start()
                rag_copy(2, s).start()
            each(body)

    def right_last(at):
        @pl.when(place == 5 - at)
        def _():
            def body(s):
                rag_wait(0, s)
                rag_copy(1, s).start()
            each(body)

    each(right_third)
    flow_first(0)
    left_step(2)
    flow_first(1)
    left_step(3)
    flow_first(2)

    def z_copy(s):
        return copy(zout.at[s], zin.at[s], lz_s.at[s], lz_r.at[s], z_far)

    def left_reduced(s):
        lrs_copy(3, s).wait_recv()
        lrs_copy(6, s).wait_recv()
        delta = ((lroot(s)[0] - y) * way + Y) % Y
        near = (delta > 0).astype(jnp.int32) * (delta < 4).astype(jnp.int32)
        zout[s] = pick((delta == 0, own[s, y]), (near == 1, lrs[6, s]), (delta >= 4, lrs[3, s]))
        z_copy(s).start()
    each(left_reduced)

    flow_second(3)
    flow_second(4)

    def lag_copy(k, s):
        block = (y - k * way + Y) % Y if k < 4 else (y + (k - 4) * way + Y) % Y
        place_ = left.at[s, core * Y + block]
        return copy(place_, place_, lag_s.at[k, s], lag_r.at[k, s], y_fwd if k < 4 else y_back)

    def lag_wait(k, s):
        block = (y - (k + 1) * way + 2 * Y) % Y if k < 4 else (y + (k - 3) * way + Y) % Y
        place_ = left.at[s, core * Y + block]
        copy(place_, place_, lag_s.at[k, s], lag_r.at[k, s], y_fwd).wait_recv()

    def block_of(j):
        return (y - j * way + Y) % Y if j < 5 else (y + (j - 4) * way + Y) % Y

    def lic_copy(j, s):
        place_ = left.at[s, core * Y + block_of(j)]
        return copy(place_, place_, lic_s.at[j, s], lic_r.at[j, s], sibling)

    def lic_wait(j, s):
        other = (y + j * way + Y) % Y if j < 5 else (y - (j - 4) * way + Y) % Y
        place_ = left.at[s, (1 - core) * Y + other]
        copy(place_, place_, lic_s.at[j, s], lic_r.at[j, s], sibling).wait_recv()

    def left_gather0(s):
        z_copy(s).wait_recv()
        root = lroot(s)[1]
        left[s, core * Y + y] = pick((root == zh, zout[s]), (root != zh, zin[s]))
        lag_copy(0, s).start()
        lag_copy(4, s).start()
        lic_copy(0, s).start()
    each(left_gather0)

    def left_gather(h):
        def body(s):
            lag_wait(h - 1, s)
            if h < 4:
                lag_copy(h, s).start()
            if h < 4:
                lag_wait(3 + h, s)
                if h < 3:
                    lag_copy(4 + h, s).start()
            lic_copy(h, s).start()
            if h < 4:
                lic_copy(4 + h, s).start()
        each(body)

    left_gather(1)
    flow_second(5)
    right_last(3)
    right_last(4)
    left_gather(2)
    right_last(5)
    left_gather(3)
    left_gather(4)

    def finish(s):
        rag_wait(1, s)
        rag_wait(2, s)
        for j in range(8):
            lic_wait(j, s)
    each(finish)

    def rows_of(i, carry):
        lhs = jnp.concatenate(
            [left[s, pl.ds(4 * i, 4)].reshape(TILE, TILE) for s in range(SECTIONS)], axis=1
        )
        rhs = right[...].reshape(SECTIONS * TILE, WIDTH)
        out[pl.ds(pl.multiple_of(i * TILE, TILE), TILE), :] = jnp.dot(
            lhs, rhs, preferred_element_type=jnp.float32
        ).astype(jnp.bfloat16)
        return carry
    lax.fori_loop(0, 4, rows_of, 0)

    def drain(s):
        sib_copy(s).wait_send()
        z_copy(s).wait_send()
        for k in range(7):
            lrs_copy(k, s).wait_send()
            lag_copy(k, s).wait_send()
        for j in range(8):
            lic_copy(j, s).wait_send()
        for k in range(3):
            rrs_copy(k, s).wait_send()
            rag_copy(k, s).wait_send()
        flood_copy(first, s, 1 - 2 * first).wait_send()

        @pl.when(place > 0)
        def _():
            flood_copy(second, s, 2 * first - 1).wait_send()
    each(drain)


def shards(values, pattern, sections):
    bf = jnp.bfloat16
    S = SECTIONS
    dma = pltpu.SemaphoreType.DMA
    return pl.pallas_call(
        kernel,
        name="exposure",
        out_shape=jax.ShapeDtypeStruct(values.shape, bf),
        in_specs=[
            pl.BlockSpec(memory_space=pltpu.SMEM),
            pl.BlockSpec(memory_space=pltpu.SMEM),
            pl.BlockSpec(memory_space=pl.ANY),
        ],
        out_specs=pl.BlockSpec(memory_space=pltpu.VMEM),
        scratch_shapes=[
            pltpu.VMEM((1024, WIDTH), bf),
            pltpu.VMEM((S, Y, LB, TILE), bf),
            pltpu.VMEM((S, Y, LB, TILE), bf),
            pltpu.VMEM((S, Y, LB, TILE), bf),
            pltpu.VMEM((7, S, LB, TILE), bf),
            pltpu.VMEM((S, LB, TILE), bf),
            pltpu.VMEM((S, LB, TILE), bf),
            pltpu.VMEM((S, 2 * Y, LB, TILE), bf),
            pltpu.VMEM((S, X, RB, WIDTH), bf),
            pltpu.VMEM((3, S, RB, WIDTH), bf),
            pltpu.VMEM((S, RB, WIDTH), bf),
            pltpu.VMEM((2, S, RB, WIDTH), bf),
            pltpu.VMEM((S, X, RB, WIDTH), bf),
            dma,
            dma((S,)), dma((S,)),
            dma((7, S)), dma((7, S)),
            dma((S,)), dma((S,)),
            dma((7, S)), dma((7, S)),
            dma((8, S)), dma((8, S)),
            dma((3, S)), dma((3, S)),
            dma((2, S)), dma((2, S)),
            dma((3, S)), dma((3, S)),
        ],
        compiler_params=pltpu.CompilerParams(
            collective_id=0, has_side_effects=True, vmem_limit_bytes=40 << 20
        ),
        cost_estimate=pl.CostEstimate(
            flops=2 * 1024 * 1024 * 768, bytes_accessed=2 * 1024 * 768 * 2, transcendentals=0
        ),
    )(sections, pattern, values)


def solution(mesh):
    in_specs = (P("row", "col"), P("row", "col"), P())
    out_specs = P("row", "col")
    return jax.shard_map(shards, mesh=mesh, in_specs=in_specs, out_specs=out_specs, check_vma=False)
```

time: 813 us -> 89.2 us (0.11)
  the two profiles are of different devices: /device:TPU:66 before, /device:TPU:1 now
where the time goes in v1:
time: 89.2 us; the launch traced here: 87.4 us
  Pallas kernels  83.5 us (94%)
  local copies, waits for them, and re-layouts  3.89 us (4%)
    pallas_call x1, Pallas kernels, shards(): pl.pallas_call(kernel, name='exposure', out_shape=jax.ShapeDtypeStruct(va...  83.5 us
    unnamed x7, local copies, waits for them, and re-layouts  3.89 us

profile of v1, /device:TPU:1, one launch (start us, length us, event | category | flops | bytes accessed | tf_op | source)
XLA Modules:
  0.0 87.4 jit_solution(17534078501937999926)
XLA Ops:
  0.0 0.0 copy-start
  0.0 1.4 %copy-done = bf16[1024,768]{1,0:T(8,128)(2,1)S(1)} copy-done((bf16[1024,768]{1,0:T(8,128)(2,1)S(1)}, bf16[1024,768]{1,0:T(8,128)(2,1)}, u32[]{:S(2)}) %copy-start) | copy-done | bytes 1572888
  1.4 0.0 copy-start.1
  1.4 0.7 copy-done.1
  2.1 0.0 copy-start.2
  2.1 0.7 copy-done.2
  2.7 83.5 %exposure.1 = bf16[1024,768]{1,0:T(8,128)(2,1)S(1)} custom-call(s32[4]{0:T(128)S(1)} %copy-done.2, s32[4,3]{1,0:T(4,128)S(1)} %copy-done.1, bf16[1024,768]{1,0:T(8,128)(2,1)S(1)} %copy-done), custom_call_target="tpu_custom_call" | custom-call | flops 1610612736 | bytes 3145728 | tf_op jit(solution)/shard_map/exposure/pallas_call | solution.py:368
  86.3 1.1 %copy.5 = bf16[1024,768]{1,0:T(8,128)(2,1)} copy(bf16[1024,768]{1,0:T(8,128)(2,1)S(1)} %exposure.1) | data formatting | bytes 3145728
Async XLA Ops:
  0.0 1.4 %copy-start = (bf16[1024,768]{1,0:T(8,128)(2,1)S(1)}, bf16[1024,768]{1,0:T(8,128)(2,1)}, u32[]{:S(2)}) copy-start(bf16[1024,768]{1,0:T(8,128)(2,1)} %values.1) | copy-start | bytes 4718596
  1.4 0.7 copy-start.1
  2.1 0.7 copy-start.2

commit v2 on v0

v2 whole, which is shorter than its diff:
```python
import jax
import jax.numpy as jnp
from jax import lax
from jax.experimental import pallas as pl
from jax.experimental.pallas import tpu as pltpu
from jax.sharding import PartitionSpec as P

TILE = 256
SECTIONS = 4
CHUNKS = 8
X, Y, ZL, ZH, CORES = 4, 8, 6, 2, 2
LB = 64
RB = 64
WIDTH = 768
MESH = pl.DeviceIdType.MESH


XC, LRS, LZ, LAG, LIC, RX, RRS, RFL, RAG, RIC = range(10)


def kernel(
    sections_any, pattern_any, values, out,
    sections, pattern, vals, product,
    sib_out, sib_in, own, lrs, zout, zin, left, ship, rown, rrs, rgot, flood, right,
    load_sems, out_sem, sent, result_r, cross_r, z_r, reduce_r, gather_r,
):
    row, col = lax.axis_index("row"), lax.axis_index("col")
    x, zl = row % X, row // X
    core, zh, y = col % CORES, col // CORES % ZH, col // (CORES * ZH)
    first = zl // 3
    place = (1 - first) * zl + first * (ZL - 1 - zl)
    second = 1 - first

    def device(dx=0, dy=0, dzl=0, dzh=0, dcore=0):
        r = (zl + dzl) * X + (x + dx + X) % X
        c = ((y + dy + Y) % Y) * (ZH * CORES) + (zh + dzh) % ZH * CORES + (core + dcore) % CORES
        return (r, c)

    def copy(src, dst, send, recv, to):
        return pltpu.make_async_remote_copy(
            src_ref=src, dst_ref=dst, send_sem=send, recv_sem=recv, device_id=to, device_id_type=MESH
        )

    def way(q):
        return 1 - 2 * (q % 2)

    sibling = device(dcore=1)
    barrier = pltpu.get_barrier_semaphore()

    def greet(to):
        pl.semaphore_signal(barrier, inc=1, device_id=to, device_id_type=MESH)

    loads = [
        pltpu.make_async_copy(src, dst, load_sems.at[i])
        for i, (src, dst) in enumerate(((values, vals), (sections_any, sections), (pattern_any, pattern)))
    ]
    for load in loads:
        load.start()
    greet(sibling)

    @pl.when(core == 0)
    def _():
        greet(device(dy=1))
        greet(device(dy=-1))
        greet(device(dzh=1))

    @pl.when(core == 1)
    def _():
        greet(device(dx=1))
        greet(device(dx=-1))

        @pl.when(zl > 0)
        def _():
            greet(device(dzl=-1))

        @pl.when(zl < ZL - 1)
        def _():
            greet(device(dzl=1))

    for load in loads:
        load.wait()

    def loop(low, high, body):
        def step(q, carry):
            body(q)
            return carry
        lax.fori_loop(low, high, step, 0)

    def each(body):
        loop(0, CHUNKS, body)

    def lroot(q):
        c = sections[q % SECTIONS] // 3
        return c // (CORES * ZH), c // CORES % ZH, c % CORES

    def rroot(q):
        r = sections[q % SECTIONS] // 4
        return r % X, r // X

    def factor(condition, scale=1):
        return (condition.astype(jnp.int32) * scale).astype(jnp.float32).astype(jnp.bfloat16)

    def pick(*choices):
        total = None
        for condition, array in choices:
            term = array * factor(condition)
            total = term if total is None else total + term
        return total

    def left_piece(dst, q):
        lc = sections[q % SECTIONS] % 3
        half = q // SECTIONS

        def block(b):
            rows = pl.ds(pl.multiple_of(half * 512 + b * LB, LB), LB)
            total = None
            for k in range(3):
                term = vals[rows, k * TILE : (k + 1) * TILE] * factor(
                    lc == k, pattern[half * 2 + b // 4, k]
                )
                total = term if total is None else total + term
            dst[q, b] = total
        loop(0, Y, block)

    def right_piece(dst, s):
        lr = sections[s] % 4
        for k in range(3):
            lanes = slice(k * TILE, (k + 1) * TILE)
            factors = [factor(lr == r, pattern[r, k]) for r in range(4)]

            def block(b):
                total = None
                for r in range(4):
                    rows = pl.ds(pl.multiple_of(r * TILE + b * RB, RB), RB)
                    term = vals[rows, lanes] * factors[r]
                    total = term if total is None else total + term
                dst[s, b, :, lanes] = total
            loop(0, X, block)

    def left_ship(q):
        return copy(sib_out.at[q], sib_in.at[q], sent.at[XC], cross_r.at[q], sibling)

    def right_ship(s):
        return copy(ship.at[s], rown.at[SECTIONS + s], sent.at[RX], cross_r.at[s], sibling)

    def block_of(j, q):
        return (y - j * way(q) + Y) % Y if j < 5 else (y + (j - 4) * way(q) + Y) % Y

    def lic_copy(j, q):
        spot = left.at[q, block_of(j, q)]
        return copy(spot, spot, sent.at[LIC], result_r, sibling)

    def ric_copy(j, q):
        block = (x + [0, -1, 2, 1][j] * way(q) + X) % X
        spot = right.at[q, block]
        return copy(spot, spot, sent.at[RIC], result_r, sibling)

    def lrs_copy(k, q):
        w = way(q)
        if k == 0:
            src = own.at[q, (y + 4) % Y]
        elif k == 4:
            src = own.at[q, (y - 3 * w + Y) % Y]
        else:
            src = lrs.at[k - 1, q]
        to = device(dy=w) if k < 4 else device(dy=-w)
        return copy(src, lrs.at[k, q], sent.at[LRS], reduce_r.at[k, q], to)

    def z_copy(q):
        return copy(zout.at[q], zin.at[q], sent.at[LZ], z_r.at[q], device(dzh=1))

    def lag_copy(k, q):
        w = way(q)
        block = (y - k * w + Y) % Y if k < 4 else (y + (k - 4) * w + Y) % Y
        spot = left.at[q, block]
        to = device(dy=w) if k < 4 else device(dy=-w)
        return copy(spot, spot, sent.at[LAG], gather_r.at[k, q], to)

    def lag_wait(k, q):
        w = way(q)
        block = (y - (k + 1) * w + Y) % Y if k < 4 else (y + (k - 3) * w + Y) % Y
        spot = left.at[q, block]
        copy(spot, spot, sent.at[LAG], gather_r.at[k, q], sibling).wait_recv()

    def rrs_copy(k, q):
        w = way(q)
        if k == 0:
            src = rown.at[q, (x + 2) % X]
        elif k == 1:
            src = rrs.at[0, q]
        else:
            src = rown.at[q, (x - w + X) % X]
        to = device(dx=w) if k < 2 else device(dx=-w)
        return copy(src, rrs.at[k, q], sent.at[RRS], reduce_r.at[k, q], to)

    def flood_copy(k, q):
        spot = flood.at[k, q]
        return copy(spot, spot, sent.at[RFL], reduce_r.at[3 + k, q], device(dzl=1 - 2 * k))

    def rag_copy(k, q):
        w = way(q)
        block = (x - w + X) % X if k == 1 else x
        spot = right.at[q, block]
        to = device(dx=-w) if k == 2 else device(dx=w)
        return copy(spot, spot, sent.at[RAG], gather_r.at[k, q], to)

    def rag_wait(k, q):
        block = (x + [-1, 2, 1][k] * way(q) + X) % X
        spot = right.at[q, block]
        copy(spot, spot, sent.at[RAG], gather_r.at[k, q], sibling).wait_recv()

    def received(ref):
        copy(ref, ref, sent.at[LIC], result_r, sibling).wait_recv()

    def drain(kind, ref):
        copy(ref, ref, sent.at[kind], result_r, sibling).wait_send()

    @pl.when(core == 0)
    def _():
        right_piece(ship, 0)
        pl.semaphore_wait(barrier, 4)

        def begin(s):
            @pl.when(s > 0)
            def _():
                right_piece(ship, s)
            right_ship(s).start()
            left_piece(own, s)
            left_piece(own, s + SECTIONS)
        loop(0, SECTIONS, begin)

        def reduce_first(q):
            left_ship(q).wait_recv()
            root = lroot(q)[2]

            def block(b):
                own[q, b] = pick((root == 0, own[q, b]), (root == 1, sib_in[q, b]))
            loop(0, Y, block)
            lrs_copy(0, q).start()
            lrs_copy(4, q).start()
        each(reduce_first)

        for h in range(1, 4):
            def reduce_next(q, h=h):
                w = way(q)
                root = lroot(q)[0]
                lrs_copy(h - 1, q).wait_recv()
                lrs[h - 1, q] = pick(
                    (root == y, own[q, (y + (4 - h) * w + Y) % Y]), (root != y, lrs[h - 1, q])
                )
                lrs_copy(h, q).start()
                if h < 3:
                    lrs_copy(3 + h, q).wait_recv()
                    lrs[3 + h, q] = pick(
                        (root == y, own[q, (y - (3 - h) * w + Y) % Y]), (root != y, lrs[3 + h, q])
                    )
                    lrs_copy(4 + h, q).start()
            each(reduce_next)

        def reduce_last(q):
            lrs_copy(3, q).wait_recv()
            lrs_copy(6, q).wait_recv()
            delta = ((lroot(q)[0] - y) * way(q) + Y) % Y
            near = (delta > 0).astype(jnp.int32) * (delta < 4).astype(jnp.int32)
            zout[q] = pick((delta == 0, own[q, y]), (near == 1, lrs[6, q]), (delta >= 4, lrs[3, q]))
            z_copy(q).start()
        each(reduce_last)

        def gather_first(q):
            z_copy(q).wait_recv()
            root = lroot(q)[1]
            left[q, y] = pick((root == zh, zout[q]), (root != zh, zin[q]))
            lag_copy(0, q).start()
            lag_copy(4, q).start()
            lic_copy(0, q).start()
        each(gather_first)

        for h in range(1, 5):
            def gather_next(q, h=h):
                lag_wait(h - 1, q)
                if h < 4:
                    lag_copy(h, q).start()
                    lag_wait(3 + h, q)
                    if h < 3:
                        lag_copy(4 + h, q).start()
                    lic_copy(4 + h, q).start()
                lic_copy(h, q).start()
            each(gather_next)

        received(right.at[pl.ds(SECTIONS, SECTIONS)])

    @pl.when(core == 1)
    def _():
        left_piece(sib_out, 0)
        up = (zl > 0).astype(jnp.int32) + (zl < ZL - 1).astype(jnp.int32)
        pl.semaphore_wait(barrier, 3 + up)

        def begin(s):
            @pl.when(s > 0)
            def _():
                left_piece(sib_out, s)
            left_ship(s).start()
            right_piece(rown, s)
            rrs_copy(0, s).start()
            left_piece(sib_out, s + SECTIONS)
            left_ship(s + SECTIONS).start()
        loop(0, SECTIONS, begin)

        def shipped(s):
            right_ship(s).wait_recv()
            rrs_copy(0, s + SECTIONS).start()
        loop(0, SECTIONS, shipped)

        def reduce_next(q):
            root = rroot(q)[0]
            rrs_copy(0, q).wait_recv()
            rrs[0, q] = pick((root == x, rown[q, (x + way(q) + X) % X]), (root != x, rrs[0, q]))
            rrs_copy(1, q).start()
            rrs_copy(2, q).start()

        def reduce_last(q):
            rrs_copy(1, q).wait_recv()
            rrs_copy(2, q).wait_recv()
            delta = ((rroot(q)[0] - x) * way(q) + X) % X
            rgot[q] = pick((delta == 0, rown[q, x]), (delta == 1, rrs[2, q]), (delta >= 2, rrs[1, q]))

        def flow_first(q):
            @pl.when(place == 0)
            def _():
                flood[first, q] = rgot[q]

            @pl.when(place > 0)
            def _():
                flood_copy(first, q).wait_recv()
                root = rroot(q)[1]
                flood[first, q] = pick((root == zl, rgot[q]), (root != zl, flood[first, q]))
            flood_copy(first, q).start()

        def flow_second(q):
            flood_copy(second, q).wait_recv()
            root = rroot(q)[1]
            flood[second, q] = pick((root == zl, rgot[q]), (root != zl, flood[second, q]))

            @pl.when(place > 0)
            def _():
                flood_copy(second, q).start()
            right[q, x] = pick((root <= zl, flood[0, q]), (root > zl, flood[1, q]))
            rag_copy(0, q).start()
            rag_copy(2, q).start()

            @pl.when(q >= SECTIONS)
            def _():
                ric_copy(0, q).start()

        def gather_next(q):
            rag_wait(0, q)
            rag_copy(1, q).start()

            @pl.when(q >= SECTIONS)
            def _():
                ric_copy(1, q).start()

        def gather_last(q):
            rag_wait(2, q)

            @pl.when(q >= SECTIONS)
            def _():
                ric_copy(3, q).start()
            rag_wait(1, q)

            @pl.when(q >= SECTIONS)
            def _():
                ric_copy(2, q).start()

        lag_first = 3 + (5 * place + 1) // 2
        lag_second = 3 + (5 * (5 - place) + 1) // 2

        def step(t):
            for lag, body in (
                (0, reduce_next),
                (3, reduce_last),
                (lag_first, flow_first),
                (lag_second, flow_second),
                (lag_second + 3, gather_next),
                (lag_second + 6, gather_last),
            ):
                @pl.when((t >= lag) & (t < lag + CHUNKS))
                def _(body=body, lag=lag):
                    body(t - lag)
        loop(0, CHUNKS + 22, step)

        received(left)

    def rows_of(i):
        lhs = jnp.concatenate(
            [
                left[i // 2 * SECTIONS + s, pl.ds(i % 2 * 4, 4)].reshape(TILE, TILE)
                for s in range(SECTIONS)
            ],
            axis=1,
        )
        rhs = right[pl.ds((1 - core) * SECTIONS, SECTIONS)].reshape(SECTIONS * TILE, WIDTH)
        rows = pl.ds(pl.multiple_of(i * TILE, TILE), TILE)
        product[rows, :] = jnp.dot(lhs, rhs, preferred_element_type=jnp.float32).astype(jnp.bfloat16)
        pltpu.make_async_copy(product.at[rows], out.at[rows], out_sem).start()
    loop(0, 4, rows_of)

    @pl.when(core == 0)
    def _():
        drain(RX, ship)
        drain(LRS, lrs)
        drain(LZ, zout)
        drain(LAG, left.at[:, pl.ds(0, 7)])
        drain(LIC, left)

    @pl.when(core == 1)
    def _():
        drain(XC, sib_out)
        drain(RRS, rrs)
        drain(RFL, flood.at[first])

        @pl.when(place > 0)
        def _():
            drain(RFL, flood.at[second])
        drain(RAG, right.at[:, pl.ds(0, 3)])
        drain(RIC, right.at[pl.ds(SECTIONS, SECTIONS)])

    pltpu.make_async_copy(product, out, out_sem).wait()


def shards(values, pattern, sections):
    bf = jnp.bfloat16
    S, C = SECTIONS, CHUNKS
    dma = pltpu.SemaphoreType.DMA
    return pl.pallas_call(
        kernel,
        name="exposure",
        out_shape=jax.ShapeDtypeStruct(values.shape, bf),
        in_specs=[
            pl.BlockSpec(memory_space=pl.ANY),
            pl.BlockSpec(memory_space=pl.ANY),
            pl.BlockSpec(memory_space=pl.ANY),
        ],
        out_specs=pl.BlockSpec(memory_space=pl.ANY),
        scratch_shapes=[
            pltpu.SMEM((S,), jnp.int32),
            pltpu.SMEM((4, 3), jnp.int32),
            pltpu.VMEM((1024, WIDTH), bf),
            pltpu.VMEM((1024, WIDTH), bf),
            pltpu.VMEM((C, Y, LB, TILE), bf),
            pltpu.VMEM((C, Y, LB, TILE), bf),
            pltpu.VMEM((C, Y, LB, TILE), bf),
            pltpu.VMEM((7, C, LB, TILE), bf),
            pltpu.VMEM((C, LB, TILE), bf),
            pltpu.VMEM((C, LB, TILE), bf),
            pltpu.VMEM((C, Y, LB, TILE), bf),
            pltpu.VMEM((S, X, RB, WIDTH), bf),
            pltpu.VMEM((C, X, RB, WIDTH), bf),
            pltpu.VMEM((3, C, RB, WIDTH), bf),
            pltpu.VMEM((C, RB, WIDTH), bf),
            pltpu.VMEM((2, C, RB, WIDTH), bf),
            pltpu.VMEM((C, X, RB, WIDTH), bf),
            dma((3,)), dma, dma((10,)), dma, dma((C,)), dma((C,)), dma((7, C)), dma((7, C)),
        ],
        compiler_params=pltpu.CompilerParams(
            collective_id=0, has_side_effects=True, vmem_limit_bytes=60 << 20
        ),
        cost_estimate=pl.CostEstimate(
            flops=2 * 1024 * 1024 * 768, bytes_accessed=2 * 1024 * 768 * 2, transcendentals=0
        ),
    )(sections, pattern, values)


def solution(mesh):
    in_specs = (P("row", "col"), P("row", "col"), P())
    out_specs = P("row", "col")
    return jax.shard_map(shards, mesh=mesh, in_specs=in_specs, out_specs=out_specs, check_vma=False)
```

time: 813 us -> 72.5 us (0.09)
  the two profiles are of different devices: /device:TPU:66 before, /device:TPU:1 now
where the time goes in v2:
time: 72.5 us; the launch traced here: 72.4 us
  Pallas kernels  69.7 us (96%)
  local copies, waits for them, and re-layouts  2.65 us (4%)
    pallas_call x1, Pallas kernels, shards(): pl.pallas_call(kernel, name='exposure', out_shape=jax.ShapeDtypeStruct(va...  69.7 us
    unnamed x1, local copies, waits for them, and re-layouts  2.65 us

profile of v2, /device:TPU:1, one launch (start us, length us, event | category | flops | bytes accessed | tf_op | source)
XLA Modules:
  0.0 72.4 jit_solution(1910249386020755593)
XLA Ops:
  0.0 69.7 %exposure.1 = bf16[1024,768]{1,0:T(8,128)(2,1)} custom-call(s32[4]{0:T(128)} %sections_any.1, s32[4,3]{1,0:T(4,128)} %pattern_any.1, bf16[1024,768]{1,0:T(8,128)(2,1)} %values.1), custom_call_target="tpu_custom_call" | custom-call | flops 1610612736 | bytes 3145728 | tf_op jit(solution)/shard_map/exposure/pallas_call | solution.py:435
  69.7 2.7 %copy.5 = bf16[1024,768]{1,0:T(8,128)(2,1)} copy(bf16[1024,768]{1,0:T(8,128)(2,1)} %exposure.1) | data formatting | bytes 3145728

commit v3 on v2

v3 whole, which is shorter than its diff:
```python
import jax
import jax.numpy as jnp
from jax import lax
from jax.experimental import pallas as pl
from jax.experimental.pallas import tpu as pltpu
from jax.sharding import PartitionSpec as P

TILE = 256
SECTIONS = 4
CHUNKS = 8
PIECES = 16
X, Y, ZL, ZH, CORES = 4, 8, 6, 2, 2
LB = 64
ORDER = (4, 3, -3, 2, -2, 1, -1, 0)
RB = 32
WIDTH = 768
MESH = pl.DeviceIdType.MESH


XC, LRS, LZ, LAG, LIC, RX, RRS, RFL, RAG, RIC = range(10)


def kernel(
    sections_any, pattern_any, values, out,
    sections, pattern, table, pieces, vals, product,
    sib_out, sib_in, own, lrs, zout, zin, left, ship, rown, rrs, rgot, flood, right,
    load_sems, out_sem, sent, result_r, cross_r, z_r, reduce_r, gather_r, along_r,
):
    row, col = lax.axis_index("row"), lax.axis_index("col")
    x, zl = row % X, row // X
    core, zh, y = col % CORES, col // CORES % ZH, col // (CORES * ZH)
    first = zl // 3
    place = (1 - first) * zl + first * (ZL - 1 - zl)
    second = 1 - first

    def device(dx=0, dy=0, dzl=0, dzh=0, dcore=0):
        r = (zl + dzl) * X + (x + dx + X) % X
        c = ((y + dy + Y) % Y) * (ZH * CORES) + (zh + dzh) % ZH * CORES + (core + dcore) % CORES
        return (r, c)

    def copy(src, dst, send, recv, to):
        return pltpu.make_async_remote_copy(
            src_ref=src, dst_ref=dst, send_sem=send, recv_sem=recv, device_id=to, device_id_type=MESH
        )

    on_y = {d: device(dy=d) for d in (-1, 1)}
    on_x = {d: device(dx=d) for d in (-1, 1)}
    z_far = device(dzh=1)
    yb = {d: (y + d + Y) % Y for d in range(-4, 5)}
    xb = {d: (x + d + X) % X for d in range(-2, 3)}

    class Chunk:
        def __init__(self, index, way):
            self.index, self.way = index, way

    sibling = device(dcore=1)
    barrier = pltpu.get_barrier_semaphore()

    def greet(to):
        pl.semaphore_signal(barrier, inc=1, device_id=to, device_id_type=MESH)

    loads = [
        pltpu.make_async_copy(src, dst, load_sems.at[i])
        for i, (src, dst) in enumerate(((values, vals), (sections_any, sections), (pattern_any, pattern)))
    ]
    for load in loads:
        load.start()
    greet(sibling)

    @pl.when(core == 0)
    def _():
        greet(on_y[1])
        greet(on_y[-1])
        greet(z_far)

    @pl.when(core == 1)
    def _():
        greet(on_x[1])
        greet(on_x[-1])

        @pl.when(zl > 0)
        def _():
            greet(device(dzl=-1))

        @pl.when(zl < ZL - 1)
        def _():
            greet(device(dzl=1))

    for load in loads:
        load.wait()

    def loop(low, high, body):
        def step(q, carry):
            body(q)
            return carry
        lax.fori_loop(low, high, step, 0)

    def each(body, low=0, high=CHUNKS):
        def pair(i):
            for parity in range(2):
                body(Chunk(2 * i + parity, 1 - 2 * parity))
        loop(low // 2, high // 2, pair)

    def tabulate(s):
        c, r = sections[s] // 3, sections[s] // 4
        entries = (c // (CORES * ZH), c // CORES % ZH, c % CORES, r % X, r // X)
        for i, entry in enumerate(entries):
            table[i, s] = entry
            table[i, s + SECTIONS] = entry
            pieces[i, 2 * s] = entry
            pieces[i, 2 * s + 1] = entry
            pieces[i, 2 * s + CHUNKS] = entry
            pieces[i, 2 * s + 1 + CHUNKS] = entry
    loop(0, SECTIONS, tabulate)

    def factor(condition, scale=1):
        return (condition.astype(jnp.int32) * scale).astype(jnp.float32).astype(jnp.bfloat16)

    def pick(*choices):
        total = None
        for condition, array in choices:
            term = array * factor(condition)
            total = term if total is None else total + term
        return total

    def left_block(dst, d):
        b = yb[d]

        def chunk(q):
            lc = sections[q % SECTIONS] % 3
            half = q // SECTIONS
            rows = pl.ds(pl.multiple_of(half * 512 + b * LB, LB), LB)
            total = None
            for k in range(3):
                term = vals[rows, k * TILE : (k + 1) * TILE] * factor(
                    lc == k, pattern[half * 2 + b // 4, k]
                )
                total = term if total is None else total + term
            dst[b, q] = total
        loop(0, CHUNKS, chunk)

    def right_piece(dst, q):
        s, half = q // 2, q % 2
        lr = sections[s] % 4
        for k in range(3):
            lanes = slice(k * TILE, (k + 1) * TILE)
            factors = [factor(lr == r, pattern[r, k]) for r in range(4)]

            def block(b):
                total = None
                for r in range(4):
                    start = r * TILE + half * (TILE // 2) + b * RB
                    term = vals[pl.ds(pl.multiple_of(start, RB), RB), lanes] * factors[r]
                    total = term if total is None else total + term
                dst[q, b, :, lanes] = total
            loop(0, X, block)

    def left_ship(d):
        b, i = yb[d], ORDER.index(d)
        return copy(sib_out.at[b], sib_in.at[b], sent.at[XC], cross_r.at[i], sibling)

    def right_ship(s):
        return copy(ship.at[s], rown.at[CHUNKS + s], sent.at[RX], cross_r.at[s], sibling)

    def block_of(j, w):
        return yb[-j * w] if j < 5 else yb[(j - 4) * w]

    def lic_copy(j, chunk):
        spot = left.at[chunk.index, block_of(j, chunk.way)]
        return copy(spot, spot, sent.at[LIC], result_r.at[chunk.index // SECTIONS], sibling)

    def ric_copy(j, chunk):
        spot = right.at[chunk.index, xb[(0, -1, 2, 1)[j] * chunk.way]]
        return copy(spot, spot, sent.at[RIC], result_r.at[0], sibling)

    def lrs_copy(k, chunk):
        q, w = chunk.index, chunk.way
        if k == 0:
            src = own.at[yb[4], q]
        elif k == 4:
            src = own.at[yb[-3 * w], q]
        else:
            src = lrs.at[k - 1, q]
        to = on_y[w] if k < 4 else on_y[-w]
        return copy(src, lrs.at[k, q], sent.at[LRS], reduce_r.at[k, q], to)

    def z_copy(chunk):
        q = chunk.index
        return copy(zout.at[q], zin.at[q], sent.at[LZ], z_r.at[q], z_far)

    def lag_copy(k, chunk):
        q, w = chunk.index, chunk.way
        spot = left.at[q, yb[-k * w] if k < 4 else yb[(k - 4) * w]]
        to = on_y[w] if k < 4 else on_y[-w]
        return copy(spot, spot, sent.at[LAG], gather_r.at[k, q], to)

    def lag_wait(k, chunk):
        q, w = chunk.index, chunk.way
        spot = left.at[q, yb[-(k + 1) * w] if k < 4 else yb[(k - 3) * w]]
        copy(spot, spot, sent.at[LAG], gather_r.at[k, q], sibling).wait_recv()

    def rrs_copy(k, chunk):
        q, w = chunk.index, chunk.way
        if k == 0:
            src = rown.at[q, xb[2]]
        elif k == 1:
            src = rrs.at[0, q]
        else:
            src = rown.at[q, xb[-w]]
        to = on_x[w] if k < 2 else on_x[-w]
        return copy(src, rrs.at[k, q], sent.at[RRS], along_r.at[k, q], to)

    first_to = device(dzl=1 - 2 * first)
    second_to = device(dzl=2 * first - 1)

    def flood_copy(k, chunk):
        q = chunk.index
        spot = flood.at[k, q]
        to = first_to if k is first else second_to
        return copy(spot, spot, sent.at[RFL], along_r.at[3 + k, q], to)

    def rag_copy(k, chunk):
        q, w = chunk.index, chunk.way
        spot = right.at[q, xb[-w] if k == 1 else x]
        to = on_x[-w] if k == 2 else on_x[w]
        return copy(spot, spot, sent.at[RAG], along_r.at[5 + k, q], to)

    def rag_wait(k, chunk):
        q, w = chunk.index, chunk.way
        spot = right.at[q, xb[(-1, 2, 1)[k] * w]]
        copy(spot, spot, sent.at[RAG], along_r.at[5 + k, q], sibling).wait_recv()

    def received(part, ref):
        copy(ref, ref, sent.at[LIC], result_r.at[part], sibling).wait_recv()

    def drain(kind, ref):
        copy(ref, ref, sent.at[kind], result_r.at[0], sibling).wait_send()

    @pl.when(core == 0)
    def _():
        for d in ORDER[:3]:
            left_block(own, d)
        pl.semaphore_wait(barrier, 4)
        for d in ORDER[:3]:
            left_ship(d).wait_recv()

        def reduce_first(chunk):
            q = chunk.index
            here, there = factor(table[2, q] == 0), factor(table[2, q] == 1)
            for k, d in ((0, 4), (4, -3 * chunk.way)):
                own[yb[d], q] = own[yb[d], q] * here + sib_in[yb[d], q] * there
                lrs_copy(k, chunk).start()
        each(reduce_first)

        def begin(s):
            right_piece(ship, s)
            right_ship(s).start()
        loop(0, CHUNKS, begin)
        for d in ORDER[3:]:
            left_block(own, d)

        def merge(q, d, got):
            mine = (table[0, q] == y).astype(jnp.int32)
            here, there = factor(table[2, q] == 0, mine), factor(table[2, q] == 1, mine)
            return own[yb[d], q] * here + sib_in[yb[d], q] * there + got * factor(mine == 0)

        for h in range(1, 4):
            if h < 3:
                left_ship(3 - h).wait_recv()
                left_ship(h - 3).wait_recv()

            def reduce_next(chunk, h=h):
                q, w = chunk.index, chunk.way
                lrs_copy(h - 1, chunk).wait_recv()
                lrs[h - 1, q] = merge(q, (4 - h) * w, lrs[h - 1, q])
                lrs_copy(h, chunk).start()
                if h < 3:
                    lrs_copy(3 + h, chunk).wait_recv()
                    lrs[3 + h, q] = merge(q, -(3 - h) * w, lrs[3 + h, q])
                    lrs_copy(4 + h, chunk).start()
            each(reduce_next)
        left_ship(0).wait_recv()

        def reduce_last(chunk):
            q, w = chunk.index, chunk.way
            delta = ((table[0, q] - y) * w + Y) % Y
            near = (delta > 0).astype(jnp.int32) * (delta < 4).astype(jnp.int32)
            lrs_copy(6, chunk).wait_recv()
            lrs_copy(3, chunk).wait_recv()
            far = lrs[6, q] * factor(near == 1) + lrs[3, q] * factor(delta >= 4)
            zout[q] = merge(q, 0, far)
            z_copy(chunk).start()
        each(reduce_last)

        def gather_first(chunk):
            q = chunk.index
            root = table[1, q]
            mine, other = factor(root == zh), factor(root != zh)
            z_copy(chunk).wait_recv()
            left[q, y] = zout[q] * mine + zin[q] * other
            lag_copy(0, chunk).start()
            lag_copy(4, chunk).start()
            lic_copy(0, chunk).start()
        each(gather_first)

        for h in range(1, 5):
            def gather_next(chunk, h=h):
                lag_wait(h - 1, chunk)
                if h < 4:
                    lag_copy(h, chunk).start()
                    lag_wait(3 + h, chunk)
                    if h < 3:
                        lag_copy(4 + h, chunk).start()
                    lic_copy(4 + h, chunk).start()
                lic_copy(h, chunk).start()
            each(gather_next)

        received(0, right.at[pl.ds(CHUNKS, CHUNKS)])

    @pl.when(core == 1)
    def _():
        left_block(sib_out, ORDER[0])
        up = (zl > 0).astype(jnp.int32) + (zl < ZL - 1).astype(jnp.int32)
        pl.semaphore_wait(barrier, 3 + up)

        for i, d in enumerate(ORDER):
            if i > 0:
                left_block(sib_out, d)
            left_ship(d).start()
            if i < 2:
                continue
            for q in ((0, 1), (2, 3), (4,), (5,), (6,), (7,))[i - 2]:
                right_piece(rown, q)
                rrs_copy(0, Chunk(q, 1 - 2 * (q % 2))).start()

        def shipped(chunk):
            right_ship(chunk.index - CHUNKS).wait_recv()
            rrs_copy(0, chunk).start()
        each(shipped, CHUNKS, PIECES)

        def reduce_next(chunk):
            q, w = chunk.index, chunk.way
            root = pieces[3, q]
            mine, other = factor(root == x), factor(root != x)
            rrs_copy(0, chunk).wait_recv()
            rrs[0, q] = rown[q, xb[w]] * mine + rrs[0, q] * other
            rrs_copy(1, chunk).start()
            rrs_copy(2, chunk).start()

        def reduce_last(chunk):
            q = chunk.index
            delta = ((pieces[3, q] - x) * chunk.way + X) % X
            rrs_copy(2, chunk).wait_recv()
            rrs_copy(1, chunk).wait_recv()
            rgot[q] = pick((delta == 0, rown[q, x]), (delta == 1, rrs[2, q]), (delta >= 2, rrs[1, q]))

        def flow_first(chunk):
            q = chunk.index

            @pl.when(place == 0)
            def _():
                flood[first, q] = rgot[q]

            @pl.when(place > 0)
            def _():
                root = pieces[4, q]
                mine, other = factor(root == zl), factor(root != zl)
                flood_copy(first, chunk).wait_recv()
                flood[first, q] = rgot[q] * mine + flood[first, q] * other
            flood_copy(first, chunk).start()

        def flow_second(chunk):
            q = chunk.index
            root = pieces[4, q]
            mine, other = factor(root == zl), factor(root != zl)
            flood_copy(second, chunk).wait_recv()
            flood[second, q] = rgot[q] * mine + flood[second, q] * other

            @pl.when(place > 0)
            def _():
                flood_copy(second, chunk).start()
            right[q, x] = pick((root <= zl, flood[0, q]), (root > zl, flood[1, q]))
            rag_copy(0, chunk).start()
            rag_copy(2, chunk).start()

            @pl.when(q >= CHUNKS)
            def _():
                ric_copy(0, chunk).start()

        def gather_next(chunk):
            rag_wait(0, chunk)
            rag_copy(1, chunk).start()

            @pl.when(chunk.index >= CHUNKS)
            def _():
                ric_copy(1, chunk).start()

        def gather_last(chunk):
            rag_wait(2, chunk)
            rag_wait(1, chunk)

            @pl.when(chunk.index >= CHUNKS)
            def _():
                ric_copy(3, chunk).start()
                ric_copy(2, chunk).start()

        lag_first = 8 + 4 * place
        lag_second = 8 + 4 * (5 - place)

        def step(u):
            for parity in range(2):
                t = 2 * u + parity
                for lag, body in (
                    (0, reduce_next),
                    (8, reduce_last),
                    (lag_first, flow_first),
                    (lag_second, flow_second),
                    (lag_second + 8, gather_next),
                    (lag_second + 16, gather_last),
                ):
                    @pl.when((t >= lag) & (t < lag + PIECES))
                    def _(body=body, lag=lag, t=t, parity=parity):
                        body(Chunk(t - lag, 1 - 2 * parity))
        loop(0, (PIECES + 44) // 2, step)


    def rows_of(i):
        lhs = jnp.concatenate(
            [
                left[i // 2 * SECTIONS + s, pl.ds(i % 2 * 4, 4)].reshape(TILE, TILE)
                for s in range(SECTIONS)
            ],
            axis=1,
        )
        rhs = right[pl.ds((1 - core) * CHUNKS, CHUNKS)].reshape(SECTIONS * TILE, WIDTH)
        rows = pl.ds(pl.multiple_of(i * TILE, TILE), TILE)
        product[rows, :] = jnp.dot(lhs, rhs, preferred_element_type=jnp.float32).astype(jnp.bfloat16)
        pltpu.make_async_copy(product.at[rows], out.at[rows], out_sem).start()
    for half in range(2):
        @pl.when(core == 1)
        def _(half=half):
            received(half, left.at[pl.ds(half * SECTIONS, SECTIONS)])
        loop(2 * half, 2 * half + 2, rows_of)

    @pl.when(core == 0)
    def _():
        drain(RX, ship)
        drain(LRS, lrs)
        drain(LZ, zout)
        drain(LAG, left.at[:, pl.ds(0, 7)])
        drain(LIC, left)

    @pl.when(core == 1)
    def _():
        drain(XC, sib_out)
        drain(RRS, rrs)
        drain(RFL, flood.at[first])

        @pl.when(place > 0)
        def _():
            drain(RFL, flood.at[second])
        drain(RAG, right.at[:, pl.ds(0, 3)])
        drain(RIC, right.at[pl.ds(CHUNKS, CHUNKS)])

    pltpu.make_async_copy(product, out, out_sem).wait()


def shards(values, pattern, sections):
    bf = jnp.bfloat16
    S, C = SECTIONS, CHUNKS
    dma = pltpu.SemaphoreType.DMA
    return pl.pallas_call(
        kernel,
        name="exposure",
        out_shape=jax.ShapeDtypeStruct(values.shape, bf),
        in_specs=[
            pl.BlockSpec(memory_space=pl.ANY),
            pl.BlockSpec(memory_space=pl.ANY),
            pl.BlockSpec(memory_space=pl.ANY),
        ],
        out_specs=pl.BlockSpec(memory_space=pl.ANY),
        scratch_shapes=[
            pltpu.SMEM((S,), jnp.int32),
            pltpu.SMEM((4, 3), jnp.int32),
            pltpu.SMEM((5, C), jnp.int32),
            pltpu.SMEM((5, PIECES), jnp.int32),
            pltpu.VMEM((1024, WIDTH), bf),
            pltpu.VMEM((1024, WIDTH), bf),
            pltpu.VMEM((Y, C, LB, TILE), bf),
            pltpu.VMEM((Y, C, LB, TILE), bf),
            pltpu.VMEM((Y, C, LB, TILE), bf),
            pltpu.VMEM((7, C, LB, TILE), bf),
            pltpu.VMEM((C, LB, TILE), bf),
            pltpu.VMEM((C, LB, TILE), bf),
            pltpu.VMEM((C, Y, LB, TILE), bf),
            pltpu.VMEM((C, X, RB, WIDTH), bf),
            pltpu.VMEM((PIECES, X, RB, WIDTH), bf),
            pltpu.VMEM((3, PIECES, RB, WIDTH), bf),
            pltpu.VMEM((PIECES, RB, WIDTH), bf),
            pltpu.VMEM((2, PIECES, RB, WIDTH), bf),
            pltpu.VMEM((PIECES, X, RB, WIDTH), bf),
            dma((3,)), dma, dma((10,)), dma((2,)), dma((C,)), dma((C,)), dma((7, C)), dma((7, C)),
            dma((8, PIECES)),
        ],
        compiler_params=pltpu.CompilerParams(
            collective_id=0, has_side_effects=True, vmem_limit_bytes=60 << 20
        ),
        cost_estimate=pl.CostEstimate(
            flops=2 * 1024 * 1024 * 768, bytes_accessed=2 * 1024 * 768 * 2, transcendentals=0
        ),
    )(sections, pattern, values)


def solution(mesh):
    in_specs = (P("row", "col"), P("row", "col"), P())
    out_specs = P("row", "col")
    return jax.shard_map(shards, mesh=mesh, in_specs=in_specs, out_specs=out_specs, check_vma=False)
```

time: 72.5 us -> 69.2 us (0.954)
  Pallas kernels: 69.7 us -> 66.4 us
    pallas_call x1, Pallas kernels: 69.7 us -> 66.4 us  [shards(): pl.pallas_call(kernel, name='exposure', out_shape=jax.ShapeDtypeStruct(va...]
where the time goes in v3:
time: 69.2 us; the launch traced here: 69 us
  Pallas kernels  66.4 us (96%)
  local copies, waits for them, and re-layouts  2.65 us (4%)
    pallas_call x1, Pallas kernels, shards(): pl.pallas_call(kernel, name='exposure', out_shape=jax.ShapeDtypeStruct(va...  66.4 us
    unnamed x1, local copies, waits for them, and re-layouts  2.65 us

profile of v3, /device:TPU:1, one launch (start us, length us, event | category | flops | bytes accessed | tf_op | source)
XLA Modules:
  0.0 69.0 jit_solution(2751156445341660197)
XLA Ops:
  0.0 66.4 %exposure.1 = bf16[1024,768]{1,0:T(8,128)(2,1)} custom-call(s32[4]{0:T(128)} %sections_any.1, s32[4,3]{1,0:T(4,128)} %pattern_any.1, bf16[1024,768]{1,0:T(8,128)(2,1)} %values.1), custom_call_target="tpu_custom_call" | custom-call | flops 1610612736 | bytes 3145728 | tf_op jit(solution)/shard_map/exposure/pallas_call | solution.py:472
  66.4 2.7 %copy.5 = bf16[1024,768]{1,0:T(8,128)(2,1)} copy(bf16[1024,768]{1,0:T(8,128)(2,1)} %exposure.1) | data formatting | bytes 3145728

commit v4 on v3

--- a/solution.py
+++ b/solution.py
@@ -24,7 +24,7 @@
     sections_any, pattern_any, values, out,
     sections, pattern, table, pieces, vals, product,
     sib_out, sib_in, own, lrs, zout, zin, left, ship, rown, rrs, rgot, flood, right,
-    load_sems, out_sem, sent, result_r, cross_r, z_r, reduce_r, gather_r, along_r,
+    load_sems, out_sem, sent, result_r, cross_r, z_r, along_r,
 ):
     row, col = lax.axis_index("row"), lax.axis_index("col")
     x, zl = row % X, row // X
@@ -182,7 +182,7 @@
         else:
             src = lrs.at[k - 1, q]
         to = on_y[w] if k < 4 else on_y[-w]
-        return copy(src, lrs.at[k, q], sent.at[LRS], reduce_r.at[k, q], to)
+        return copy(src, lrs.at[k, q], sent.at[LRS], along_r.at[k, q], to)
 
     def z_copy(chunk):
         q = chunk.index
@@ -192,12 +192,12 @@
         q, w = chunk.index, chunk.way
         spot = left.at[q, yb[-k * w] if k < 4 else yb[(k - 4) * w]]
         to = on_y[w] if k < 4 else on_y[-w]
-        return copy(spot, spot, sent.at[LAG], gather_r.at[k, q], to)
+        return copy(spot, spot, sent.at[LAG], along_r.at[k, CHUNKS + q], to)
 
     def lag_wait(k, chunk):
         q, w = chunk.index, chunk.way
         spot = left.at[q, yb[-(k + 1) * w] if k < 4 else yb[(k - 3) * w]]
-        copy(spot, spot, sent.at[LAG], gather_r.at[k, q], sibling).wait_recv()
+        copy(spot, spot, sent.at[LAG], along_r.at[k, CHUNKS + q], sibling).wait_recv()
 
     def rrs_copy(k, chunk):
         q, w = chunk.index, chunk.way
@@ -499,8 +499,7 @@
             pltpu.VMEM((PIECES, RB, WIDTH), bf),
             pltpu.VMEM((2, PIECES, RB, WIDTH), bf),
             pltpu.VMEM((PIECES, X, RB, WIDTH), bf),
-            dma((3,)), dma, dma((10,)), dma((2,)), dma((C,)), dma((C,)), dma((7, C)), dma((7, C)),
-            dma((8, PIECES)),
+            dma((3,)), dma, dma((10,)), dma((2,)), dma((C,)), dma((C,)), dma((8, PIECES)),
         ],
         compiler_params=pltpu.CompilerParams(
             collective_id=0, has_side_effects=True, vmem_limit_bytes=60 << 20

time: 69.2 us -> 68.2 us (0.986)
  Pallas kernels: 66.4 us -> 65.4 us
    pallas_call x1, Pallas kernels: 66.4 us -> 65.4 us  [shards(): pl.pallas_call(kernel, name='exposure', out_shape=jax.ShapeDtypeStruct(va...]
where the time goes in v4:
time: 68.2 us; the launch traced here: 68 us
  Pallas kernels  65.4 us (96%)
  local copies, waits for them, and re-layouts  2.65 us (4%)
    pallas_call x1, Pallas kernels, shards(): pl.pallas_call(kernel, name='exposure', out_shape=jax.ShapeDtypeStruct(va...  65.4 us
    unnamed x1, local copies, waits for them, and re-layouts  2.65 us

profile of v4, /device:TPU:1, one launch (start us, length us, event | category | flops | bytes accessed | tf_op | source)
XLA Modules:
  0.0 68.0 jit_solution(13722445859593208462)
XLA Ops:
  0.0 65.4 %exposure.1 = bf16[1024,768]{1,0:T(8,128)(2,1)} custom-call(s32[4]{0:T(128)} %sections_any.1, s32[4,3]{1,0:T(4,128)} %pattern_any.1, bf16[1024,768]{1,0:T(8,128)(2,1)} %values.1), custom_call_target="tpu_custom_call" | custom-call | flops 1610612736 | bytes 3145728 | tf_op jit(solution)/shard_map/exposure/pallas_call | solution.py:472
  65.4 2.7 %copy.5 = bf16[1024,768]{1,0:T(8,128)(2,1)} copy(bf16[1024,768]{1,0:T(8,128)(2,1)} %exposure.1) | data formatting | bytes 3145728
